TPU v7x, 32 devices: a whole 2x2x4 slice. The times are simulated.
32 devices in a mesh: grp: 2 (over x), space: 16 (over z, y, core).
Axes of the slice: x: 2, y: 2, z: 4, core: 2. Of those that a mesh axis runs over, the one named last changes fastest.
Arguments:
- inputs: bfloat16 [96, 128, 128, 128], P('grp', 'space'), parts along dimension 0, may hold values from -6 to 6
- cotangent: bfloat16 [96, 128, 128, 128], P('grp', 'space'), parts along dimension 0, may hold values from -6 to 6
- spectral_weight: bfloat16 [256, 16, 2, 2304], P('space'), may hold values from -20 to 20
- pointwise_weight: bfloat16 [48, 48], replicated, may hold values from -0.875 to 0.875
- bias: float32 [48], replicated, may hold values from -3 to 3
Outputs:
- grad_input: bfloat16 [96, 128, 128, 128], P('grp', 'space'), parts along dimension 0
- grad_spectral: float32 [512, 16, 2, 2304], P(('grp', 'space')), parts along dimension 0
- grad_pointwise: float32 [96, 48], P('grp'), parts along dimension 0
- grad_bias: float32 [96], P('grp'), parts along dimension 0
There are 2 independent parts, one for each index of `grp`. A program takes and returns all parts, laid end to end along the dimension named above; an argument that names none is the same for every part. Nothing has to cross between parts.
All inputs are finite; a program needn't handle non-finite values.
Results may differ from a plain program's by a relative error of at most 0.0075.
Values sent between devices are 32-bit elements; how exact they have to be, the bound alone decides.
A program may use at most 192 MiB of HBM per device.

v0:
```python
import math

import jax
import jax.numpy as jnp
from jax import lax
from jax.sharding import PartitionSpec as P

N = 128
M = 16


HIGH = lax.Precision.HIGHEST


def phases(positions, freqs, length):
    product = positions[:, None] * freqs[None, :] % length
    angle = product.astype(jnp.float32) * (2.0 * math.pi / length)
    return (jnp.cos(angle), jnp.sin(angle))


def x_forward(real_part, imag_part, cosine, sine):
    ur = jnp.einsum("cxp,xm->pmc", real_part, cosine, precision=HIGH) + jnp.einsum(
        "cxp,xm->pmc", imag_part, sine, precision=HIGH
    )
    ui = jnp.einsum("cxp,xm->pmc", imag_part, cosine, precision=HIGH) - jnp.einsum(
        "cxp,xm->pmc", real_part, sine, precision=HIGH
    )
    return jnp.stack([ur, ui], 2)


def x_inverse(modes, cosine, sine):
    wr = modes[:, :, 0]
    wi = modes[:, :, 1]
    qr = jnp.einsum("pmc,xm->cxp", wr, cosine, precision=HIGH) - jnp.einsum(
        "pmc,xm->cxp", wi, sine, precision=HIGH
    )
    qi = jnp.einsum("pmc,xm->cxp", wr, sine, precision=HIGH) + jnp.einsum(
        "pmc,xm->cxp", wi, cosine, precision=HIGH
    )
    return jnp.stack([qr, qi], 1)


def yz_forward(section, cosine, sine):
    real_part = section[:, :M]
    imag_part = section[:, M:]
    y_real = jnp.einsum("ckxy,yj->cxjk", real_part, cosine, precision=HIGH) + jnp.einsum(
        "ckxy,yj->cxjk", imag_part, sine, precision=HIGH
    )
    y_imag = jnp.einsum("ckxy,yj->cxjk", imag_part, cosine, precision=HIGH) - jnp.einsum(
        "ckxy,yj->cxjk", real_part, sine, precision=HIGH
    )
    channels, planes = (y_real.shape[0], y_real.shape[1])
    return jnp.stack(
        [y_real.reshape(channels, planes, M * M), y_imag.reshape(channels, planes, M * M)], 1
    )


def yz_inverse(stacked, cosine, sine):
    channels, planes = (stacked.shape[0], stacked.shape[2])
    qr = stacked[:, 0].reshape(channels, planes, M, M)
    qi = stacked[:, 1].reshape(channels, planes, M, M)
    rr = jnp.einsum("cxjk,yj->cxyk", qr, cosine, precision=HIGH) - jnp.einsum(
        "cxjk,yj->cxyk", qi, sine, precision=HIGH
    )
    ri = jnp.einsum("cxjk,yj->cxyk", qr, sine, precision=HIGH) + jnp.einsum(
        "cxjk,yj->cxyk", qi, cosine, precision=HIGH
    )
    table = jnp.concatenate([cosine.T, -sine.T], 0)
    return jnp.einsum("cxyk,kz->cxyz", jnp.concatenate([rr, ri], 3), table, precision=HIGH)


def forward_modes(field, cosine, sine, pencils_dev):
    planes = field.shape[1]
    freqs = jnp.arange(M, dtype=jnp.int32)
    z_table = jnp.concatenate([cosine, -sine], 1).astype(jnp.bfloat16)
    section = jnp.einsum("cxyz,zk->ckxy", field, z_table, preferred_element_type=jnp.float32)
    lines = yz_forward(section, cosine, sine)
    offset = lax.axis_index("space") * planes
    local_pos = offset + jnp.arange(planes, dtype=jnp.int32)
    x_cos, x_sin = phases(local_pos, freqs, N)
    summed = lax.psum_scatter(
        x_forward(lines[:, 0], lines[:, 1], x_cos, x_sin).reshape(
            pencils_dev * lax.axis_size("space"), M * 2 * lines.shape[0]
        ),
        "space",
        scatter_dimension=0,
        tiled=True,
    )
    modes = summed.reshape(pencils_dev, M, 2, lines.shape[0])
    return modes * float(N) ** (-1.5)


def inverse_modes(modes, cosine, sine, planes):
    freqs = jnp.arange(M, dtype=jnp.int32)
    channels = modes.shape[3]
    offset = lax.axis_index("space") * planes
    local_pos = offset + jnp.arange(planes, dtype=jnp.int32)
    x_cos, x_sin = phases(local_pos, freqs, N)
    flat = modes.reshape(modes.shape[0], M * 2 * channels)
    piece = lax.all_gather(flat, "space", axis=0, tiled=True)
    count = piece.shape[0]
    local = x_inverse(piece.reshape(count, M, 2, channels), x_cos, x_sin)
    return yz_inverse(local, cosine, sine) * float(N) ** (-1.5)


def split_weight(weight, channels):
    pencils = weight.shape[0]
    wr = weight[:, :, 0].astype(jnp.float32).reshape(pencils, M, channels, channels)
    wi = weight[:, :, 1].astype(jnp.float32).reshape(pencils, M, channels, channels)
    return (wr, wi)


def activate(values):
    return jax.nn.gelu(values, approximate=True)


def per_device(inputs, cotangent, spectral_weight, pointwise_weight, bias):
    channels, planes, width = (inputs.shape[0], inputs.shape[1], inputs.shape[2])
    pencils_dev = spectral_weight.shape[0]
    cosine, sine = phases(jnp.arange(width, dtype=jnp.int32), jnp.arange(M, dtype=jnp.int32), N)
    inputs_hat = forward_modes(inputs, cosine, sine, pencils_dev)
    wr, wi = split_weight(spectral_weight, channels)
    ur, ui = (inputs_hat[:, :, 0], inputs_hat[:, :, 1])
    mr = jnp.einsum("pmi,pmio->pmo", ur, wr, precision=HIGH) - jnp.einsum(
        "pmi,pmio->pmo", ui, wi, precision=HIGH
    )
    mi = jnp.einsum("pmi,pmio->pmo", ur, wi, precision=HIGH) + jnp.einsum(
        "pmi,pmio->pmo", ui, wr, precision=HIGH
    )
    spectral = inverse_modes(jnp.stack([mr, mi], 2), cosine, sine, planes)
    linear = jnp.einsum(
        "oi,ixyz->oxyz", pointwise_weight, inputs, preferred_element_type=jnp.float32
    )
    pre = spectral + linear + bias[:, None, None, None]
    primal, pull = jax.vjp(activate, pre)
    slope = pull(cotangent.astype(jnp.float32))[0].astype(jnp.bfloat16)
    scale = float(N) ** (-1.5)
    weight_part = jnp.einsum("oxyz,ixyz->oi", slope, inputs, preferred_element_type=jnp.float32)
    bias_part = jnp.sum(slope.astype(jnp.float32), axis=(1, 2, 3))
    weight_total, bias_total = lax.psum((weight_part, bias_part), "space")
    slope_hat = forward_modes(slope, cosine, sine, pencils_dev)
    sr, si = (slope_hat[:, :, 0], slope_hat[:, :, 1])
    grad_real = jnp.einsum("pmi,pmo->pmio", ur, sr, precision=HIGH) + jnp.einsum(
        "pmi,pmo->pmio", ui, si, precision=HIGH
    )
    grad_imag = jnp.einsum("pmi,pmo->pmio", ur, si, precision=HIGH) - jnp.einsum(
        "pmi,pmo->pmio", ui, sr, precision=HIGH
    )
    grad_spectral = jnp.stack([grad_real, grad_imag], 2).reshape(
        pencils_dev, M, 2, channels * channels
    )
    back_real = jnp.einsum("pmio,pmo->pmi", wr, sr, precision=HIGH) + jnp.einsum(
        "pmio,pmo->pmi", wi, si, precision=HIGH
    )
    back_imag = jnp.einsum("pmio,pmo->pmi", wr, si, precision=HIGH) - jnp.einsum(
        "pmio,pmo->pmi", wi, sr, precision=HIGH
    )
    back_field = inverse_modes(jnp.stack([back_real, back_imag], 2), cosine, sine, planes)
    transpose_term = jnp.einsum(
        "oi,oxyz->ixyz", pointwise_weight, slope, preferred_element_type=jnp.float32
    )
    grad_input = (back_field + transpose_term).astype(jnp.bfloat16)
    return (grad_input, grad_spectral, weight_total * scale, bias_total * scale)


def solution(mesh):
    placed = (
        P("grp", "space", None, None),
        P("grp", "space", None, None),
        P("space", None, None, None),
        P(),
        P(),
    )
    return jax.shard_map(
        per_device,
        mesh=mesh,
        in_specs=placed,
        out_specs=(
            P("grp", "space", None, None),
            P(("grp", "space"), None, None, None),
            P("grp", None),
            P("grp"),
        ),
        check_vma=False,
    )
```

profile of v0, /device:TPU:0, one launch (start us, length us, event | category | flops | bytes accessed | tf_op | source)
XLA Modules:
  0.0 620.3 jit_solution(1818315345540124261)
XLA Ops:
  7.3 7.3 %convolution_bitcast_fusion.1 = f32[48,32,8,128]{3,1,2,0:T(8,128)S(1)} fusion(bf16[48,8,128,128]{3,2,1,0:T(8,128)(2,1)} %param.5, bf16[128,16]{0,1:T(8,128)(2,1)S(1)} %get-tuple-element.36, bf16[128,16]{0,1:T(8,128)(2,1)S(1)} %get-tuple-element.37), kind=kOutput, calls=%fused_computation.56 | convolution fusion | flops 402669568 | bytes 18882560 | tf_op jit(solution)/shard_map/cxyz,zk->ckxy/dot_general | solution.py:76
  15.3 11.5 %fusion.33 = f32[16,48,16,8]{1,0,3,2:T(8,128)} fusion(f32[48,16,8,128]{3,1,2,0:T(8,128)S(1)} %get-tuple-element.23), kind=kOutput, calls=%fused_computation.47 | convolution fusion | flops 151023616 | bytes 3538944 | tf_op jit(solution)/shard_map/ckxy,yj->cxjk/dot_general | solution.py:49
  26.8 11.9 %fusion.35 = f32[16,48,16,8]{1,0,3,2:T(8,128)} fusion(f32[48,16,8,128]{3,1,2,0:T(8,128)S(1)} %get-tuple-element.23), kind=kOutput, calls=%fused_computation.49 | convolution fusion | flops 151023616 | bytes 3538944 | tf_op jit(solution)/shard_map/ckxy,yj->cxjk/dot_general | solution.py:46
  38.7 13.0 %fusion.44 = f32[48,8,16,16]{0,2,1,3:T(8,128)} fusion(f32[16,48,16,8]{1,0,3,2:T(8,128)} %fusion.35, f32[48,16,8,128]{3,1,2,0:T(8,128)S(1)} %get-tuple-element.22), kind=kOutput, calls=%fused_computation.62 | convolution fusion | flops 151121920 | bytes 3932160 | tf_op jit(solution)/shard_map/ckxy,yj->cxjk/dot_general | solution.py:46
  51.7 10.5 %fusion.50 = f32[48,8,16,16]{0,2,1,3:T(8,128)S(1)} fusion(f32[16,48,16,8]{1,0,3,2:T(8,128)S(1)} %copy-done.13, f32[48,16,8,128]{3,1,2,0:T(8,128)S(1)} %get-tuple-element.22), kind=kOutput, calls=%fused_computation.64 | convolution fusion | flops 151121920 | bytes 3932160 | tf_op jit(solution)/shard_map/ckxy,yj->cxjk/dot_general | solution.py:49
  74.1 11.6 %slice_reduce_fusion.1 = (bf16[16,16,2304]{2,1,0:T(8,128)(2,1)}, bf16[16,16,2304]{2,1,0:T(8,128)(2,1)}) fusion(bf16[16,16,2,2304]{3,2,1,0:T(2,128)(2,1)S(1)} %copy-done.7), kind=kLoop, calls=%fused_computation.58 | loop fusion | bytes 4718592 | tf_op jit(solution)/shard_map/slice | solution.py:108
  91.0 6.3 %reshape.52 = bf16[16,16,48,48]{3,2,1,0:T(8,128)(2,1)} reshape(bf16[16,16,2304]{2,1,0:T(8,128)(2,1)} %get-tuple-element.17) | data formatting | bytes 2359296 | tf_op jit(solution)/shard_map/reshape | solution.py:109
  97.3 39.1 %reduce-scatter.7.cloned.1.call-done = f32[16,1536]{1,0:T(8,128)} async-done(((f32[256,1536]{1,0:T(8,128)}), f32[16,1536]{1,0:T(8,128)}) %reduce-scatter.7.cloned.1.call-update) | async-done | bytes 98320 | tf_op jit(solution)/shard_map/reduce_scatter | solution.py:81
  153.1 23.7 %fusion.17 = f32[48,8,128,128]{3,0,2,1:T(8,128)} fusion(bf16[48,8,128,128]{3,2,1,0:T(8,128)(2,1)} %param.5, bf16[48,48]{1,0:T(8,128)(2,1)S(1)} %copy-done), kind=kOutput, calls=%fused_computation.24 | convolution fusion | flops 603979776 | bytes 37753344 | tf_op jit(solution)/shard_map/oi,ixyz->oxyz/dot_general | solution.py:131
  176.8 14.9 %all-gather.3.cloned.1.call-done = f32[256,1536]{1,0:T(8,128)} async-done(((f32[16,1536]{1,0:T(8,128)}), f32[256,1536]{1,0:T(8,128)}) %all-gather.3.cloned.1.call-update) | async-done | bytes 1572880 | tf_op jit(solution)/shard_map/all_gather | solution.py:100
  234.3 64.5 %convert_reduce_fusion = (f32[48]{0:T(128)}, bf16[48,8,128,128]{3,2,1,0:T(8,128)(2,1)}) fusion(f32[48]{0:T(128)S(1)} %copy-done.22, f32[48,8,128,128]{3,0,2,1:T(8,128)} %fusion.17, f32[16,128]{1,0:T(8,128)S(1)} %get-tuple-element.38, f32[16,128]{1,0:T(8,128)S(1)} %get-tuple-element.39, f32[48,8,128,16]{2,3,1,0:T(8,128)S(1)} %add_bitcast_fusion.1, ...), kind=kOutput, calls=%fused_computation.18 | convolution fusion | flops 2581073920 | bytes 56639872 | tf_op jit(solution)/shard_map/cxyk,kz->cxyz/dot_general | solution.py:69
  298.8 7.5 %convolution_bitcast_fusion = f32[48,32,8,128]{3,1,2,0:T(8,128)S(1)} fusion(bf16[48,8,128,128]{3,2,1,0:T(8,128)(2,1)} %get-tuple-element.35, bf16[128,16]{0,1:T(8,128)(2,1)S(1)} %get-tuple-element.36, bf16[128,16]{0,1:T(8,128)(2,1)S(1)} %get-tuple-element.37), kind=kOutput, calls=%fused_computation.55 | convolution fusion | flops 402669568 | bytes 18882560 | tf_op jit(solution)/shard_map/cxyz,zk->ckxy/dot_general | solution.py:76
  307.3 10.6 %fusion.25 = f32[16,48,16,8]{1,0,3,2:T(8,128)S(1)} fusion(f32[48,16,8,128]{3,1,2,0:T(8,128)S(1)} %get-tuple-element.21), kind=kOutput, calls=%fused_computation.39 | convolution fusion | flops 151023616 | bytes 3538944 | tf_op jit(solution)/shard_map/ckxy,yj->cxjk/dot_general | solution.py:49
  317.8 10.7 %fusion.27 = f32[16,48,16,8]{1,0,3,2:T(8,128)S(1)} fusion(f32[48,16,8,128]{3,1,2,0:T(8,128)S(1)} %get-tuple-element.21), kind=kOutput, calls=%fused_computation.41 | convolution fusion | flops 151023616 | bytes 3538944 | tf_op jit(solution)/shard_map/ckxy,yj->cxjk/dot_general | solution.py:46
  328.6 12.0 %fusion.56 = f32[48,8,16,16]{0,2,1,3:T(8,128)} fusion(f32[16,48,16,8]{1,0,3,2:T(8,128)S(1)} %fusion.27, f32[48,16,8,128]{3,1,2,0:T(8,128)S(1)} %get-tuple-element.20), kind=kOutput, calls=%fused_computation.66 | convolution fusion | flops 151121920 | bytes 3932160 | tf_op jit(solution)/shard_map/ckxy,yj->cxjk/dot_general | solution.py:46
  340.6 10.5 %fusion.62 = f32[48,8,16,16]{0,2,1,3:T(8,128)S(1)} fusion(f32[16,48,16,8]{1,0,3,2:T(8,128)S(1)} %fusion.25, f32[48,16,8,128]{3,1,2,0:T(8,128)S(1)} %get-tuple-element.20), kind=kOutput, calls=%fused_computation.68 | convolution fusion | flops 151121920 | bytes 3932160 | tf_op jit(solution)/shard_map/ckxy,yj->cxjk/dot_general | solution.py:49
  373.3 22.5 %fusion.73 = f32[48,48]{1,0:T(8,128)S(1)} fusion(bf16[48,8,128,128]{3,2,1,0:T(8,128)(2,1)} %param.5, bf16[48,8,128,128]{3,2,1,0:T(8,128)(2,1)} %get-tuple-element.35), kind=kOutput, calls=%fused_computation.85 | convolution fusion | flops 603979776 | bytes 25175040 | tf_op jit(solution)/shard_map/oxyz,ixyz->oi/dot_general | solution.py:138
  395.8 59.6 %all-reduce = (f32[48,48]{1,0:T(8,128)S(1)}, f32[48]{0:T(128)S(1)}) all-reduce(f32[48,48]{1,0:T(8,128)S(1)} %fusion.73, f32[48]{0:T(128)S(1)} %copy-done.21), channel_id=1, replica_groups=mesh['grp'=2,'space'=16] {'space'}, use_global_device_ids=true, to_apply=%region_2.3 | all-reduce | flops 2352 | bytes 18816 | tf_op jit(solution)/shard_map/psum | solution.py:140
  459.4 6.7 %fusion.82 = f32[16,16,1,48]{3,2,1,0:T(1,128)S(1)} fusion(bf16[16,16,48,48]{3,2,1,0:T(8,128)(2,1)} %reshape.52, f32[16,16,2,48]{3,2,1,0:T(2,128)S(1)} %mul.327), kind=kOutput, calls=%fused_computation.96 | convolution fusion | flops 7077888 | bytes 1359872 | tf_op jit(solution)/shard_map/pmio,pmo->pmi/dot_general | solution.py:155
  482.4 23.5 %fusion.14 = f32[8,128,128,48]{2,3,1,0:T(8,128)} fusion(bf16[48,8,128,128]{3,2,1,0:T(8,128)(2,1)} %get-tuple-element.35, bf16[48,48]{1,0:T(8,128)(2,1)S(1)} %copy-done), kind=kOutput, calls=%fused_computation.21 | convolution fusion | flops 603979776 | bytes 37753344 | tf_op jit(solution)/shard_map/oi,oxyz->ixyz/dot_general | solution.py:159
  506.1 7.2 %multiply_add_fusion = (f32[16,16,48,48]{3,2,1,0:T(8,128)}, f32[16,16,48,48]{3,2,1,0:T(8,128)}) fusion(f32[16,16,48]{2,1,0:T(8,128)S(1)} %bitcast.273, f32[16,16,48]{2,1,0:T(8,128)S(1)} %bitcast.271, f32[16,16,48]{2,1,0:T(8,128)S(1)} %bitcast.272, f32[16,16,48]{2,1,0:T(8,128)S(1)} %bitcast.270), kind=kLoop, calls=%fused_computation.33 | loop fusion | flops 3538944 | bytes 4915200 | tf_op jit(solution)/shard_map/add | solution.py:143
  518.3 6.2 %stack.58 = f32[16,16,1,2304]{3,1,0,2:T(8,128)} reshape(f32[16,16,48,48]{3,2,1,0:T(8,128)} %get-tuple-element.29) | data formatting | bytes 4718592 | tf_op jit(solution)/shard_map/stack | solution.py:149
  526.8 5.8 copy.165
  566.6 47.0 %fusion.10 = bf16[48,8,128,128]{3,2,1,0:T(8,128)(2,1)} fusion(f32[8,128,128,48]{2,3,1,0:T(8,128)} %fusion.14, f32[48,8,128,16]{2,3,1,0:T(8,128)S(1)} %add_bitcast_fusion, f32[48,8,128,16]{2,3,1,0:T(8,128)S(1)} %subtract_bitcast_fusion, f32[16,128]{1,0:T(8,128)S(1)} %copy-done.18, f32[16,128]{1,0:T(8,128)S(1)} %copy-done.20), kind=kOutput, calls=%fused_computation.15 | convolution fusion | flops 2436370432 | bytes 44056576 | tf_op jit(solution)/shard_map/cxyk,kz->cxyz/dot_general | solution.py:69
  (137 shorter events, 161.7 us)
Async XLA Ops:
  7.2 145.9 %copy-start = (bf16[48,48]{1,0:T(8,128)(2,1)S(1)}, bf16[48,48]{1,0:T(8,128)(2,1)}, u32[]{:S(2)}) copy-start(bf16[48,48]{1,0:T(8,128)(2,1)} %param.8) | copy-start | bytes 13828
  7.2 129.2 %reduce-scatter.7.cloned.1.call-start = ((), (), s32[]{:S(2)}) async-start(), calls=%async_computation.4 | async-start | bytes 1671168 | tf_op jit(solution)/shard_map/reduce_scatter | solution.py:81
  38.7 13.0 %copy-start.13 = (f32[16,48,16,8]{1,0,3,2:T(8,128)S(1)}, f32[16,48,16,8]{1,0,3,2:T(8,128)}, u32[]{:S(2)}) copy-start(f32[16,48,16,8]{1,0,3,2:T(8,128)} %fusion.33) | copy-start | bytes 1179652
  70.9 3.2 copy-start.7
  74.1 117.6 %all-gather.3.cloned.1.call-start = ((), (), s32[]{:S(2)}) async-start(), calls=%async_computation.2 | async-start | bytes 1671168 | tf_op jit(solution)/shard_map/all_gather | solution.py:100
  137.8 4.3 copy-start.1
  152.8 303.8 %reduce-scatter.9.cloned.1.call-start = ((), (), s32[]{:S(2)}) async-start(), calls=%async_computation.5 | async-start | bytes 1671168 | tf_op jit(solution)/shard_map/reduce_scatter | solution.py:81
  153.1 81.2 %copy-start.17 = (f32[16,128]{1,0:T(8,128)}, f32[16,128]{1,0:T(8,128)S(1)}, u32[]{:S(2)}) copy-start(f32[16,128]{1,0:T(8,128)S(1)} %get-tuple-element.38) | copy-start | bytes 24580
  153.1 81.2 %copy-start.19 = (f32[16,128]{1,0:T(8,128)}, f32[16,128]{1,0:T(8,128)S(1)}, u32[]{:S(2)}) copy-start(f32[16,128]{1,0:T(8,128)S(1)} %get-tuple-element.39) | copy-start | bytes 24580
  207.6 5.7 copy-start.3
  213.3 4.4 copy-start.11
  213.3 4.4 copy-start.15
  226.2 5.1 copy-start.4
  226.2 5.1 copy-start.6
  231.3 3.0 copy-start.22
  360.1 6.1 copy-start.14
  372.4 160.3 %all-gather.5.cloned.1.call-start = ((), (), s32[]{:S(2)}) async-start(), calls=%async_computation.3 | async-start | bytes 1671168 | tf_op jit(solution)/shard_map/all_gather | solution.py:100
  373.3 22.5 %copy-start.21 = (f32[48]{0:T(128)S(1)}, f32[48]{0:T(128)}, u32[]{:S(2)}) copy-start(f32[48]{0:T(128)} %get-tuple-element.34) | copy-start | bytes 580
  459.4 6.7 %copy-start.2 = (bf16[16,16,48,48]{3,2,1,0:T(8,128)(2,1)S(1)}, bf16[16,16,48,48]{3,2,1,0:T(8,128)(2,1)}, u32[]{:S(2)}) copy-start(bf16[16,16,48,48]{3,2,1,0:T(8,128)(2,1)} %reshape.52) | copy-start | bytes 3538948
  482.4 23.7 %copy-start.16 = (f32[16,16,1,48]{3,2,1,0:T(1,128)S(1)}, f32[16,16,1,48]{3,2,1,0:T(1,128)}, u32[]{:S(2)}) copy-start(f32[16,16,1,48]{3,2,1,0:T(1,128)} %get-tuple-element.31) | copy-start | bytes 147460
  547.4 4.3 copy-start.9
  558.3 5.1 copy-start.5
  563.3 3.2 copy-start.18
  563.3 3.2 copy-start.20
  (3 other events, 5.9 us)
Sparse Core Ops, SparseCore 0:
  74.2 62.1 reduce-scatter.6
  152.9 38.6 all-gather.2
  372.5 58.4 reduce-scatter.8
  482.5 36.8 all-gather.4
where the time goes:
time: 631 us; the launch traced here: 620 us
  matrix products  376 us (60%)
  local copies, waits for them, and re-layouts  101 us (16%)
  blocking collectives  59.6 us (9%)
  waiting for transfers between devices  54 us (9%)
  other arithmetic  14.8 us (2%)
  between operations  14.5 us (2%)
    dot_general x2, matrix products, yz_inverse(): jnp.einsum('cxyk,kz->cxyz', jnp.concatenate([rr, ri], 3), table, precisio...  112 us
    psum x1, blocking collectives, per_device(): weight_total, bias_total = lax.psum((weight_part, bias_part), 'space')  59.6 us
    reduce_scatter x2, waiting for transfers between devices, forward_modes(): lax.psum_scatter(x_forward(lines[:, 0], lines[:, 1], x_cos, x_sin).reshap...  39.1 us
    dot_general x2, matrix products, yz_forward(): jnp.einsum('ckxy,yj->cxjk', real_part, cosine, precision=HIGH)  25 us
    dot_general x1, matrix products, per_device(): jnp.einsum('oi,ixyz->oxyz', pointwise_weight, inputs, preferred_element_t...  23.7 us
    dot_general x1, matrix products, per_device(): jnp.einsum('oi,oxyz->ixyz', pointwise_weight, slope, preferred_element_ty...  23.5 us
    dot_general x2, matrix products, yz_forward(): jnp.einsum('ckxy,yj->cxjk', imag_part, sine, precision=HIGH)  22.6 us
    dot_general x1, matrix products, per_device(): jnp.einsum('oxyz,ixyz->oi', slope, inputs, preferred_element_type=jnp.flo...  22.5 us
  transfers between devices with their start and end apart: 4, of which 2 were waited for; matrix products, arithmetic and copies ran while one was open for 20% of the time, Pallas kernels for 0%

commit v1 on v0

v1 whole, which is shorter than its diff:
```python
import functools
import math

import jax
import jax.numpy as jnp
import numpy as np
from jax import lax
from jax.experimental import pallas as pl
from jax.experimental.pallas import tpu as pltpu
from jax.sharding import PartitionSpec as P

M = 16
T16 = 16
HIGH = lax.Precision.HIGHEST
BF = jnp.bfloat16
F32 = jnp.float32
LIMIT = 56 * 1024 * 1024


class Plan:
    def __init__(self, space, channels, width):
        self.S = space
        self.C = channels
        self.N = width
        self.X = width // space
        self.h = space // M
        self.kl = M // self.h
        self.g = 4 * self.h
        self.G = channels // self.g
        self.L = 128 * self.h
        self.rows = self.X * self.G
        self.rp = -(-channels // space)
        self.rows_p = self.rows + 8
        self.pairs = channels * channels
        self.tables()

    def tables(self):
        S, C, N, h, kl, g, G, L = self.S, self.C, self.N, self.h, self.kl, self.g, self.G, self.L
        ang = 2.0 * np.pi * ((np.arange(N)[:, None] * np.arange(M)[None, :]) % N) / N
        cos, sin = np.cos(ang), np.sin(ang)
        scale = float(N) ** -1.5
        bf = lambda a: np.asarray(a, np.float32).astype(jnp.bfloat16)
        f32 = lambda a: np.asarray(a, np.float32)
        fwd = np.zeros((g, N, 2, h, 2, g, kl))
        inv = np.zeros((h, 2, g, kl, g, N))
        for c in range(g):
            for p in range(h):
                k = slice(p * kl, (p + 1) * kl)
                fwd[c, :, 0, p, 0, c] = cos[:, k]
                fwd[c, :, 0, p, 1, c] = -sin[:, k]
                fwd[c, :, 1, p, 0, c] = -sin[:, k]
                fwd[c, :, 1, p, 1, c] = -cos[:, k]
                inv[p, 0, c, :, c] = cos[:, k].T
                inv[p, 1, c, :, c] = -sin[:, k].T
        self.z_fwd = bf(fwd.reshape(g * N, 2 * L))
        self.z_inv = bf(inv.reshape(L, g * N))
        self.y_fwd = bf(np.concatenate([cos.T, sin.T], 1))
        self.y_inv = bf(np.concatenate([cos, sin], 1))
        dup = lambda a: np.repeat(a, 2, axis=0)
        self.x_fwd = f32(np.concatenate([dup(cos.T), dup(sin.T)], 0) * scale)
        self.x_inv = f32(np.concatenate([dup(cos.T).T, dup(sin.T).T], 1) * scale)
        fold = np.zeros((G, 2, g, kl, 2, 128))
        unfold = np.zeros((128, G, 2, g, kl))
        for a in range(G):
            for c in range(g):
                for r in range(2):
                    fold[a, r, c, :, r, a * g + c] = 1
                    unfold[a * g + c, a, r, c, :] = 1
        self.fold = bf(fold.reshape(G * 128, 256))
        self.unfold = bf(unfold.reshape(128, G * 128))
        e1 = np.zeros((128, C, C))
        e2 = np.zeros((128, C, C))
        for c in range(C):
            e1[c, c, :] = 1
            e2[c, :, c] = 1
        self.e1 = bf(e1.reshape(128, C * C))
        self.e2 = bf(e2.reshape(128, C * C))
        self.e1t = bf(e1.reshape(128, C * C).T)
        self.e2t = bf(e2.reshape(128, C * C).T)
        spread = np.zeros((C, T16, 128))
        for c in range(C):
            spread[c, :, c] = 1
        self.spread = bf(spread.reshape(C * T16, 128))


def dot(a, b, precision=None):
    return jnp.dot(a, b, preferred_element_type=F32, precision=precision)


def dot_t(a, b):
    return lax.dot_general(a, b, (((1,), (1,)), ((), ())), preferred_element_type=F32)


def params(**more):
    return pltpu.CompilerParams(vmem_limit_bytes=LIMIT, **more)


def lines_of(plan, plane, x, z_fwd, y_fwd, out):
    for a in range(plan.G):
        wide = jnp.concatenate([plane(a * plan.g + c) for c in range(plan.g)], axis=1)
        section = dot(wide, z_fwd[...]).astype(BF)
        both = jnp.concatenate([section[:, : plan.L], section[:, plan.L :]], axis=0)
        line = dot(y_fwd[...], both)
        for p in range(plan.h):
            out[:, p, a * plan.X + x, :] = line[:, p * 128 : (p + 1) * 128]


def field_of(plan, lines, x, y_inv, z_inv, out):
    lane = lax.broadcasted_iota(jnp.int32, (M, 128), 1)
    sign = jnp.where(lane < 64, -1.0, 1.0).astype(F32)
    for a in range(plan.G):
        parts = []
        for p in range(plan.h):
            q = lines[:, p, a * plan.X + x, :]
            turned = pltpu.roll(q, 64, 1) * sign
            parts.append(jnp.concatenate([q, turned], axis=0))
        both = jnp.concatenate(parts, axis=1).astype(BF)
        across = dot(y_inv[...], both).astype(BF)
        values = dot(across, z_inv[...])
        for c in range(plan.g):
            out[a * plan.g + c] = values[:, c * plan.N : (c + 1) * plan.N]


def first_kernel(plan, field, z_fwd, y_fwd, out):
    x = pl.program_id(0)

    @pl.when(x == 0)
    def _():
        out[:, :, plan.rows :, :] = jnp.zeros((M, plan.h, 8, 128), F32)

    lines_of(plan, lambda c: field[c, 0], x, z_fwd, y_fwd, out)


def spread_weight(plan, weight, spread):
    rows = plan.C * T16
    half = dot(spread[...], weight[...]).astype(BF)
    full = dot_t(half, spread[...])
    r = lax.broadcasted_iota(jnp.int32, (rows, rows), 0) % T16
    c = lax.broadcasted_iota(jnp.int32, (rows, rows), 1) % T16
    return jnp.where(r == c, full, 0.0)


def slope_of(pre, cot):
    k = math.sqrt(2.0 / math.pi)
    square = pre * pre
    t = jnp.tanh(pre * (k + (k * 0.044715) * square))
    inner = pre * (0.5 * k + (1.5 * k * 0.044715) * square)
    return cot * (0.5 + 0.5 * t + inner * (1.0 - t * t))


def middle_kernel(plan, lines, field, cot, weight, bias, spread, y_inv, z_inv, z_fwd, y_fwd,
                  slope, out, pre, mix, acc, bias_acc):
    x = pl.program_id(0)
    C, N = plan.C, plan.N
    rows = C * T16

    @pl.when(x == 0)
    def _():
        out[:, :, plan.rows :, :] = jnp.zeros((M, plan.h, 8, 128), F32)
        mix[...] = spread_weight(plan, weight, spread).astype(BF)
        acc[...] = jnp.zeros_like(acc)
        bias_acc[...] = jnp.zeros_like(bias_acc)

    field_of(plan, lines, x, y_inv, z_inv, pre)

    def block(b, carry):
        ys = [pl.ds(pl.multiple_of(b * 2 * T16 + i * T16, T16), T16) for i in range(2)]
        wide = jnp.concatenate([field[:, 0, y, :].reshape(rows, N) for y in ys], axis=1)
        linear = dot(mix[...], wide)
        for i, y in enumerate(ys):
            part = linear[:, i * N : (i + 1) * N].reshape(C, T16, N)
            total = part + pre[:, y, :] + bias[...]
            got = slope_of(total, cot[:, 0, y, :].astype(F32)).astype(BF)
            slope[:, 0, y, :] = got
            wider = got.astype(F32)
            bias_acc[...] += wider[:, :8] + wider[:, 8:]
        return carry

    lax.fori_loop(0, N // (2 * T16), block, 0)
    lines_of(plan, lambda c: slope[c, 0], x, z_fwd, y_fwd, out)
    tall = lambda ref: jnp.concatenate(
        [ref[:, 0, i * T16 : (i + 1) * T16, :].reshape(rows, N) for i in range(N // T16)], axis=1
    )
    acc[...] += dot_t(tall(slope), tall(field))

    @pl.when(x == pl.num_programs(0) - 1)
    def _():
        r = lax.broadcasted_iota(jnp.int32, (rows, rows), 0) % T16
        c = lax.broadcasted_iota(jnp.int32, (rows, rows), 1) % T16
        kept = jnp.where(r == c, acc[...], 0.0)
        right = dot(kept, spread[...].astype(F32), HIGH)
        pointwise = jnp.sum(right.reshape(C, T16, 128), axis=1)
        ends = jnp.sum(jnp.sum(bias_acc[...], axis=1), axis=1, keepdims=True)
        lane = lax.broadcasted_iota(jnp.int32, (C, 128), 1)
        final = jnp.where(lane == C, ends, pointwise)
        for o in range(C):
            d, row = o // plan.rp, o % plan.rp
            out[d // plan.h, d % plan.h, plan.rows + row, :] = final[o]


def last_kernel(plan, lines, slope, weight, spread, y_inv, z_inv, grad, pre, mix):
    x = pl.program_id(0)
    C, N = plan.C, plan.N
    rows = C * T16

    @pl.when(x == 0)
    def _():
        mix[...] = spread_weight(plan, weight, spread).astype(BF)

    field_of(plan, lines, x, y_inv, z_inv, pre)

    def block(b, carry):
        ys = [pl.ds(pl.multiple_of(b * 2 * T16 + i * T16, T16), T16) for i in range(2)]
        wide = jnp.concatenate([slope[:, 0, y, :].reshape(rows, N) for y in ys], axis=1)
        linear = dot(mix[...], wide)
        for i, y in enumerate(ys):
            part = linear[:, i * N : (i + 1) * N].reshape(C, T16, N)
            grad[:, 0, y, :] = (part + pre[:, y, :]).astype(BF)
        return carry

    lax.fori_loop(0, N // (2 * T16), block, 0)


def whole(shape):
    return pl.BlockSpec(shape, lambda x: (0,) * len(shape))


def plane_spec(plan):
    return pl.BlockSpec((plan.C, 1, plan.N, plan.N), lambda x: (0, x, 0, 0))


def lines_shape(plan):
    return (M, plan.h, plan.rows_p, 128)


def run_first(plan, field):
    consts = [plan.z_fwd, plan.y_fwd]
    return pl.pallas_call(
        functools.partial(first_kernel, plan),
        grid=(plan.X,),
        in_specs=[plane_spec(plan)] + [whole(c.shape) for c in consts],
        out_specs=whole(lines_shape(plan)),
        out_shape=jax.ShapeDtypeStruct(lines_shape(plan), F32),
        compiler_params=params(),
        name="first",
    )(field, *[jnp.asarray(c) for c in consts])


def pad_weight(weight):
    return jnp.pad(weight, ((0, 128 - weight.shape[0]), (0, 128 - weight.shape[1])))


def run_middle(plan, lines, field, cot, weight, bias):
    rows = plan.C * T16
    consts = [plan.spread, plan.y_inv, plan.z_inv, plan.z_fwd, plan.y_fwd]
    wide = jnp.broadcast_to(bias[:, None, None], (plan.C, 1, 128))
    return pl.pallas_call(
        functools.partial(middle_kernel, plan),
        grid=(plan.X,),
        in_specs=[
            whole(lines_shape(plan)), plane_spec(plan), plane_spec(plan),
            whole((128, 128)), whole((plan.C, 1, 128)),
        ] + [whole(c.shape) for c in consts],
        out_specs=(plane_spec(plan), whole(lines_shape(plan))),
        out_shape=(
            jax.ShapeDtypeStruct(field.shape, BF),
            jax.ShapeDtypeStruct(lines_shape(plan), F32),
        ),
        scratch_shapes=[
            pltpu.VMEM((plan.C, plan.N, plan.N), F32),
            pltpu.VMEM((rows, rows), BF),
            pltpu.VMEM((rows, rows), F32),
            pltpu.VMEM((plan.C, 8, 128), F32),
        ],
        compiler_params=params(),
        name="middle",
    )(lines, field, cot, pad_weight(weight), wide, *[jnp.asarray(c) for c in consts])


def run_last(plan, lines, slope, weight):
    rows = plan.C * T16
    consts = [plan.spread, plan.y_inv, plan.z_inv]
    return pl.pallas_call(
        functools.partial(last_kernel, plan),
        grid=(plan.X,),
        in_specs=[whole(lines_shape(plan)), plane_spec(plan), whole((128, 128))]
        + [whole(c.shape) for c in consts],
        out_specs=plane_spec(plan),
        out_shape=jax.ShapeDtypeStruct(slope.shape, BF),
        scratch_shapes=[
            pltpu.VMEM((plan.C, plan.N, plan.N), F32),
            pltpu.VMEM((rows, rows), BF),
        ],
        compiler_params=params(),
        name="last",
    )(lines, slope, pad_weight(weight.T), *[jnp.asarray(c) for c in consts])


def modes_of(plan, lines, x_fwd, fold):
    P_ = plan.kl
    lane = lax.broadcasted_iota(jnp.int32, (2 * M, 128), 1)
    sign = jnp.where(lane < 64, 1.0, -1.0).astype(F32)
    rows = lax.broadcasted_iota(jnp.int32, (P_, 2 * M, 128), 0)
    lanes = lax.broadcasted_iota(jnp.int32, (P_, 2 * M, 128), 2) % P_
    own = rows == lanes
    parts = []
    for a in range(plan.G):
        block = lines[:, a * plan.X : (a + 1) * plan.X, :].reshape(plan.N, 128)
        both = dot(x_fwd[...], block, HIGH)
        u = both[: 2 * M] + sign * pltpu.roll(both[2 * M :], 64, 1)
        picked = jnp.where(own, u[None], 0.0)
        parts.append(picked.reshape(P_ * 2 * M, 128).astype(BF))
    return dot(jnp.concatenate(parts, axis=1), fold[...])


def lines_back(plan, real, imag, back, x_inv, unfold, out):
    P_ = plan.kl
    shape = (P_, 2 * M, 128)
    lane = lax.broadcasted_iota(jnp.int32, shape, 2)
    own = lax.broadcasted_iota(jnp.int32, shape, 0) == lane % P_
    same = (lax.broadcasted_iota(jnp.int32, shape, 1) % 2) == lane // 64
    is_real = lane < 64
    if back:
        sign_a, sign_b = jnp.where(is_real, 1.0, -1.0), 1.0
    else:
        sign_a, sign_b = 1.0, jnp.where(is_real, -1.0, 1.0)
    half = lax.broadcasted_iota(jnp.int32, (2 * M, 128), 1)
    turn = jnp.where(half < 64, -1.0, 1.0).astype(F32)
    for a in range(plan.G):
        cut = unfold[:, a * 128 : (a + 1) * 128]
        ra = dot(real, cut).reshape(shape) * sign_a
        rb = dot(imag, cut).reshape(shape) * sign_b
        v = jnp.sum(jnp.where(own, jnp.where(same, ra, rb), 0.0), axis=0)
        both = jnp.concatenate([v, turn * pltpu.roll(v, 64, 1)], axis=0)
        q = dot(x_inv[...], both, HIGH)
        out[:, a * plan.X : (a + 1) * plan.X, :] = q.reshape(plan.S, plan.X, 128)


def mix_forward(plan, lines, weight, x_fwd, x_inv, fold, unfold, e1, e2t, out, modes, ab):
    modes[...] = modes_of(plan, lines, x_fwd, fold).astype(BF)

    def chunk(b, carry):
        rows = pl.ds(pl.multiple_of(b * 64, 64), 64)
        w = weight[rows, :].astype(F32)
        for part in range(2):
            wide = dot(modes[rows, part * 128 : (part + 1) * 128], e1[...])
            ab[part, rows, :] = dot((wide * w).astype(BF), e2t[...]).astype(BF)
        return carry

    lax.fori_loop(0, modes.shape[0] // 64, chunk, 0)
    lines_back(plan, ab[0], ab[1], False, x_inv, unfold, out)
    out[:, plan.rows :, :] = jnp.zeros((plan.S, 8, 128), F32)


def mix_backward(plan, lines, weight, modes, x_fwd, x_inv, fold, unfold, e1, e2, e1t,
                 out, grad, held, turned, ab):
    s = modes_of(plan, lines, x_fwd, fold)
    held[...] = s.astype(BF)
    even = lax.broadcasted_iota(jnp.int32, (s.shape[0], 128), 0) % 2 == 0
    sr, si = s[:, :128], s[:, 128:]
    turned[:, :128] = jnp.where(even, sr, si).astype(BF)
    turned[:, 128:] = jnp.where(even, si, -sr).astype(BF)

    def chunk(b, carry):
        rows = pl.ds(pl.multiple_of(b * 64, 64), 64)
        w = weight[rows, :].astype(F32)
        for part in range(2):
            wide = dot(held[rows, part * 128 : (part + 1) * 128], e2[...])
            ab[part, rows, :] = dot((wide * w).astype(BF), e1t[...]).astype(BF)
        ur = dot(modes[rows, :128], e1[...])
        first = ur * dot(turned[rows, :128], e2[...])
        ui = dot(modes[rows, 128:], e1[...])
        grad[rows, :] = first + ui * dot(turned[rows, 128:], e2[...])
        return carry

    lax.fori_loop(0, s.shape[0] // 64, chunk, 0)
    lines_back(plan, ab[0], ab[1], True, x_inv, unfold, out)
    total = jnp.sum(lines[:, plan.rows :, :], axis=0) * float(plan.N) ** -1.5
    out[:, plan.rows :, :] = jnp.broadcast_to(total[None], (plan.S, 8, 128))


def run_mix_forward(plan, lines, weight):
    rows = plan.kl * 2 * M
    consts = [plan.x_fwd, plan.x_inv, plan.fold, plan.unfold, plan.e1, plan.e2t]
    return pl.pallas_call(
        functools.partial(mix_forward, plan),
        out_shape=(
            jax.ShapeDtypeStruct((plan.S, plan.rows_p, 128), F32),
            jax.ShapeDtypeStruct((rows, 256), BF),
        ),
        scratch_shapes=[pltpu.VMEM((2, rows, 128), BF)],
        compiler_params=params(),
        name="mix_forward",
    )(lines, weight, *[jnp.asarray(c) for c in consts])


def run_mix_backward(plan, lines, weight, modes):
    rows = plan.kl * 2 * M
    consts = [plan.x_fwd, plan.x_inv, plan.fold, plan.unfold, plan.e1, plan.e2, plan.e1t]
    return pl.pallas_call(
        functools.partial(mix_backward, plan),
        out_shape=(
            jax.ShapeDtypeStruct((plan.S, plan.rows_p, 128), F32),
            jax.ShapeDtypeStruct((rows, plan.pairs), F32),
        ),
        scratch_shapes=[
            pltpu.VMEM((rows, 256), BF),
            pltpu.VMEM((rows, 256), BF),
            pltpu.VMEM((2, rows, 128), BF),
        ],
        compiler_params=params(),
        name="mix_backward",
    )(lines, weight, modes, *[jnp.asarray(c) for c in consts])


def exchange_kernel(n, src, dst, send, recv, own):
    me = lax.axis_index("space")
    barrier = pltpu.get_barrier_semaphore()
    for k in range(1, n):
        pl.semaphore_signal(barrier, inc=1, device_id={"space": lax.rem(me + k, n)},
                            device_id_type=pl.DeviceIdType.MESH)
    pl.semaphore_wait(barrier, n - 1)
    copies = []
    for k in range(1, n):
        to = lax.rem(me + k, n)
        copy = pltpu.make_async_remote_copy(
            src_ref=src.at[to], dst_ref=dst.at[me], send_sem=send.at[k], recv_sem=recv.at[k],
            device_id={"space": to}, device_id_type=pl.DeviceIdType.MESH,
        )
        copy.start()
        copies.append(copy)
    local = pltpu.make_async_copy(src.at[me], dst.at[me], own)
    local.start()
    local.wait()
    for copy in copies:
        copy.wait()


def exchange(plan, blocks):
    n = plan.S
    return pl.pallas_call(
        functools.partial(exchange_kernel, n),
        out_shape=jax.ShapeDtypeStruct(blocks.shape, blocks.dtype),
        in_specs=[pl.BlockSpec(memory_space=pl.ANY)],
        out_specs=pl.BlockSpec(memory_space=pl.ANY),
        scratch_shapes=[
            pltpu.SemaphoreType.DMA((n,)),
            pltpu.SemaphoreType.DMA((n,)),
            pltpu.SemaphoreType.DMA,
        ],
        compiler_params=pltpu.CompilerParams(collective_id=0, has_side_effects=True),
        name="exchange",
    )(blocks)


def per_device(plan, inputs, cotangent, spectral_weight, pointwise_weight, bias):
    C = plan.C
    owners = (plan.S, plan.rows_p, 128)
    weight = spectral_weight.reshape(plan.kl * 2 * M, plan.pairs)
    lines = run_first(plan, inputs)
    got = exchange(plan, lines.reshape(owners))
    back, modes = run_mix_forward(plan, got, weight)
    got = exchange(plan, back).reshape(lines_shape(plan))
    slope, lines = run_middle(plan, got, inputs, cotangent, pointwise_weight, bias)
    got = exchange(plan, lines.reshape(owners))
    back, grad = run_mix_backward(plan, got, weight, modes)
    got = exchange(plan, back)
    grad_input = run_last(plan, got.reshape(lines_shape(plan)), slope, pointwise_weight)
    small = got[:, plan.rows : plan.rows + plan.rp, :].reshape(plan.S * plan.rp, 128)[:C]
    return (
        grad_input,
        grad.reshape(plan.kl, M, 2, plan.pairs),
        small[:, :C],
        small[:, C],
    )


def solution(mesh):
    space = mesh.shape["space"]

    def run(inputs, cotangent, spectral_weight, pointwise_weight, bias):
        channels = pointwise_weight.shape[0]
        plan = Plan(space, channels, inputs.shape[2])
        return jax.shard_map(
            functools.partial(per_device, plan),
            mesh=mesh,
            in_specs=(
                P("grp", "space", None, None),
                P("grp", "space", None, None),
                P("space", None, None, None),
                P(),
                P(),
            ),
            out_specs=(
                P("grp", "space", None, None),
                P(("grp", "space"), None, None, None),
                P("grp", None),
                P("grp"),
            ),
            check_vma=False,
        )(inputs, cotangent, spectral_weight, pointwise_weight, bias)

    return run
```

time: 631 us -> 276 us (0.44); the launches traced: 620 us -> 272 us
  matrix products: 376 us -> 0 us
  Pallas kernels: 0 us -> 257 us
  local copies, waits for them, and re-layouts: 101 us -> 14.6 us
  blocking collectives: 59.6 us -> 0 us
  waiting for transfers between devices: 54 us -> 0 us
  other arithmetic: 14.8 us -> 0 us
  between operations: 14.5 us -> 0.69 us
    dot_general x47 -> x0, matrix products: 376 us -> none  [the longest x2 112 us: yz_inverse(): jnp.einsum('cxyk,kz->cxyz', jnp.concatenate([rr, ri], 3), table, precisio...]
    pallas_call x0 -> x9, Pallas kernels: none -> 257 us  [the longest x4 90.4 us: exchange(): pl.pallas_call(functools.partial(exchange_kernel, n), out_shape=jax.Shape...]
    psum x1 -> x0, blocking collectives: 59.6 us -> none  [per_device(): weight_total, bias_total = lax.psum((weight_part, bias_part), 'space')]
    reduce_scatter x2 -> x0, waiting for transfers between devices: 39.1 us -> none  [forward_modes(): lax.psum_scatter(x_forward(lines[:, 0], lines[:, 1], x_cos, x_sin).reshap...]
    another operation x12 -> x0, local copies, waits for them, and re-layouts: 38 us -> none  [the longest x2 11.2 us: per_device(): jnp.stack([grad_real, grad_imag], 2)]
    all_gather x2 -> x0, waiting for transfers between devices: 14.9 us -> none  [inverse_modes(): piece = lax.all_gather(flat, 'space', axis=0, tiled=True)]
    slice x7 -> x2, local copies, waits for them, and re-layouts: 15.9 us -> 1.54 us  [the longest x1 0.84 us: per_device(): got[:, plan.rows:plan.rows + plan.rp, :].reshape(plan.S * plan.rp, 128)[:C]]
    unnamed x49 -> x5, local copies, waits for them, and re-layouts: 12.4 us -> 0.95 us
  transfers between devices with their start and end apart: 4 -> 0, of which waited for: 2 -> 0; matrix products, arithmetic and copies ran while one was open for 20% -> 0% of each run, Pallas kernels for 0% -> 0%
where the time goes in v1:
time: 276 us; the launch traced here: 272 us
  Pallas kernels  257 us (93%)
  local copies, waits for them, and re-layouts  14.6 us (5%)
    pallas_call x4, Pallas kernels, exchange(): pl.pallas_call(functools.partial(exchange_kernel, n), out_shape=jax.Shape...  90.4 us
    pallas_call x1, Pallas kernels, run_middle(): pl.pallas_call(functools.partial(middle_kernel, plan), grid=(plan.X,), in...  80.7 us
    pallas_call x1, Pallas kernels, run_last(): pl.pallas_call(functools.partial(last_kernel, plan), grid=(plan.X,), in_s...  37.7 us
    pallas_call x1, Pallas kernels, run_first(): pl.pallas_call(functools.partial(first_kernel, plan), grid=(plan.X,), in_...  17.8 us
    pallas_call x1, Pallas kernels, run_mix_backward(): pl.pallas_call(functools.partial(mix_backward, plan), out_shape=(jax.Shap...  16.6 us
    pallas_call x1, Pallas kernels, run_mix_forward(): pl.pallas_call(functools.partial(mix_forward, plan), out_shape=(jax.Shape...  13.6 us
    reshape x1, local copies, waits for them, and re-layouts, per_device(): grad.reshape(plan.kl, M, 2, plan.pairs)  6.42 us

profile of v1, /device:TPU:0, one launch (start us, length us, event | category | flops | bytes accessed | tf_op | source)
XLA Modules:
  0.0 272.1 jit_solution(1527225450086940528)
XLA Ops:
  0.6 0.0 copy-start
  0.6 0.9 copy.23
  1.6 0.6 pad.8.weight
  2.2 1.4 broadcast_in_dim.2.bias
  3.6 1.3 pad.7.weight
  4.9 17.8 %first.1 = f32[16,1,104,128]{3,2,1,0:T(8,128)} custom-call(bf16[48,8,128,128]{3,2,1,0:T(8,128)(2,1)} %field.3, bf16[512,256]{1,0:T(8,128)(2,1)} %constant.29.clone.z_fwd, bf16[16,256]{1,0:T(8,128)(2,1)} %constant.30.clone.y_fwd), custom_call_target="tpu_custom_call" | custom-call | tf_op jit(solution)/shard_map/first/pallas_call | solution.py:238
  22.7 20.9 %exchange.4.lines = f32[16,104,128]{2,1,0:T(8,128)} custom-call(f32[16,104,128]{2,1,0:T(8,128)} %bitcast.7), custom_call_target="tpu_custom_call" | custom-call | tf_op jit(solution)/shard_map/exchange/pallas_call | solution.py:441
  43.6 0.0 copy-done
  43.6 2.3 reshape.33.weight
  45.9 13.6 %mix_forward.1 = (f32[16,104,128]{2,1,0:T(8,128)}, bf16[512,256]{1,0:T(8,128)(2,1)}) custom-call(f32[16,104,128]{2,1,0:T(8,128)} %exchange.4.lines, bf16[512,2304]{1,0:T(8,128)(2,1)} %reshape.33.weight, f32[64,128]{1,0:T(8,128)} %constant.31.clone.x_fwd, f32[128,64]{1,0:T(8,128)} %constant.32.clone.x_inv, bf16[1536,256]{1,0:T(8,128)(2,1)} %constant.33.clone.fold, ...), custom_call_target="tpu_custom_call" | custom-call | tf_op jit(solution)/shard_map/mix_forward/pallas_call | solution.py:385
  59.6 23.1 %exchange.5 = f32[16,104,128]{2,1,0:T(8,128)} custom-call(f32[16,104,128]{2,1,0:T(8,128)} %get-tuple-element.10.src), custom_call_target="tpu_custom_call" | custom-call | tf_op jit(solution)/shard_map/exchange/pallas_call | solution.py:441
  82.7 80.7 %middle.1 = (bf16[48,8,128,128]{3,2,1,0:T(8,128)(2,1)}, f32[16,1,104,128]{3,2,1,0:T(8,128)}) custom-call(f32[16,1,104,128]{3,2,1,0:T(8,128)} %bitcast.8, bf16[48,8,128,128]{3,2,1,0:T(8,128)(2,1)} %field.3, bf16[48,8,128,128]{3,2,1,0:T(8,128)(2,1)} %cot.1, bf16[128,128]{1,0:T(8,128)(2,1)} %pad.7.weight, f32[48,1,128]{2,1,0:T(1,128)} %broadcast_in_dim.2.bias, ...), custom_call_target="tpu_custom_call" | custom-call | tf_op jit(solution)/shard_map/middle/pallas_call | solution.py:257
  163.4 23.2 %exchange.6.lines = f32[16,104,128]{2,1,0:T(8,128)} custom-call(f32[16,104,128]{2,1,0:T(8,128)} %bitcast.9), custom_call_target="tpu_custom_call" | custom-call | tf_op jit(solution)/shard_map/exchange/pallas_call | solution.py:441
  186.6 16.6 %mix_backward.1 = (f32[16,104,128]{2,1,0:T(8,128)}, f32[512,2304]{1,0:T(8,128)}) custom-call(f32[16,104,128]{2,1,0:T(8,128)} %exchange.6.lines, bf16[512,2304]{1,0:T(8,128)(2,1)} %reshape.33.weight, bf16[512,256]{1,0:T(8,128)(2,1)} %get-tuple-element.12.modes, f32[64,128]{1,0:T(8,128)} %constant.31.clone.x_fwd, f32[128,64]{1,0:T(8,128)} %constant.32.clone.x_inv, ...), custom_call_target="tpu_custom_call" | custom-call | tf_op jit(solution)/shard_map/mix_backward/pallas_call | solution.py:400
  203.2 23.2 %exchange.7 = f32[16,104,128]{2,1,0:T(8,128)} custom-call(f32[16,104,128]{2,1,0:T(8,128)} %get-tuple-element.13.src), custom_call_target="tpu_custom_call" | custom-call | tf_op jit(solution)/shard_map/exchange/pallas_call | solution.py:441
  226.4 37.7 %last.1 = bf16[48,8,128,128]{3,2,1,0:T(8,128)(2,1)} custom-call(f32[16,1,104,128]{3,2,1,0:T(8,128)} %bitcast.6, bf16[48,8,128,128]{3,2,1,0:T(8,128)(2,1)} %get-tuple-element.14.slope, bf16[128,128]{1,0:T(8,128)(2,1)} %pad.8.weight, bf16[768,128]{1,0:T(8,128)(2,1)} %constant.37.clone.spread, bf16[128,32]{1,0:T(8,128)(2,1)} %constant.38.clone.y_inv, ...), custom_call_target="tpu_custom_call" | custom-call | tf_op jit(solution)/shard_map/last/pallas_call | solution.py:283
  264.1 0.8 slice.9
  264.9 0.0 copy-start.1
  265.0 0.7 slice_reduce_fusion
  265.7 6.4 %reshape.37 = f32[16,16,2,2304]{3,2,1,0:T(2,128)} reshape(f32[512,2304]{1,0:T(8,128)} %get-tuple-element.15) | data formatting | bytes 9437184 | tf_op jit(solution)/shard_map/reshape | solution.py:472
  272.1 0.0 copy-done.1
  (1 shorter events, 0.0 us)
Async XLA Ops:
  0.6 43.0 %copy-start = (bf16[16,16,2,2304]{3,2,1,0:T(2,128)(2,1)S(1)}, bf16[16,16,2,2304]{3,2,1,0:T(2,128)(2,1)}, u32[]{:S(2)}) copy-start(bf16[16,16,2,2304]{3,2,1,0:T(2,128)(2,1)} %param.20) | copy-start | bytes 7077892
  264.9 7.1 %copy-start.1 = (f32[48,128]{1,0:T(8,128)}, f32[48,128]{1,0:T(8,128)S(1)}, u32[]{:S(2)}) copy-start(f32[48,128]{1,0:T(8,128)S(1)} %reshape.38) | copy-start | bytes 73732

commit v2 on v1

--- a/solution.py
+++ b/solution.py
@@ -96,45 +96,68 @@
 
 
 def lines_of(plan, plane, x, z_fwd, y_fwd, out):
-    for a in range(plan.G):
-        wide = jnp.concatenate([plane(a * plan.g + c) for c in range(plan.g)], axis=1)
+    size = plan.G // 3
+    for start in range(0, plan.G, size):
+        wide = jnp.concatenate(
+            [
+                jnp.concatenate([plane(a * plan.g + c) for c in range(plan.g)], axis=1)
+                for a in range(start, start + size)
+            ],
+            axis=0,
+        )
         section = dot(wide, z_fwd[...]).astype(BF)
-        both = jnp.concatenate([section[:, : plan.L], section[:, plan.L :]], axis=0)
+        both = jnp.concatenate(
+            [
+                jnp.concatenate(
+                    [section[i * plan.N : (i + 1) * plan.N, r * plan.L : (r + 1) * plan.L]
+                     for i in range(size)],
+                    axis=1,
+                )
+                for r in range(2)
+            ],
+            axis=0,
+        )
         line = dot(y_fwd[...], both)
-        for p in range(plan.h):
-            out[:, p, a * plan.X + x, :] = line[:, p * 128 : (p + 1) * 128]
+        for i in range(size):
+            for p in range(plan.h):
+                at = i * plan.L + p * 128
+                out[:, p, (start + i) * plan.X + x, :] = line[:, at : at + 128]
 
 
 def field_of(plan, lines, x, y_inv, z_inv, out):
     lane = lax.broadcasted_iota(jnp.int32, (M, 128), 1)
     sign = jnp.where(lane < 64, -1.0, 1.0).astype(F32)
-    for a in range(plan.G):
+    size = plan.G // 3
+    for start in range(0, plan.G, size):
         parts = []
-        for p in range(plan.h):
-            q = lines[:, p, a * plan.X + x, :]
-            turned = pltpu.roll(q, 64, 1) * sign
-            parts.append(jnp.concatenate([q, turned], axis=0))
+        for i in range(size):
+            for p in range(plan.h):
+                q = lines[:, p, (start + i) * plan.X + x, :]
+                turned = pltpu.roll(q, 64, 1) * sign
+                parts.append(jnp.concatenate([q, turned], axis=0))
         both = jnp.concatenate(parts, axis=1).astype(BF)
         across = dot(y_inv[...], both).astype(BF)
-        values = dot(across, z_inv[...])
-        for c in range(plan.g):
-            out[a * plan.g + c] = values[:, c * plan.N : (c + 1) * plan.N]
+        tall = jnp.concatenate(
+            [across[:, i * plan.L : (i + 1) * plan.L] for i in range(size)], axis=0
+        )
+        values = dot(tall, z_inv[...])
+        for i in range(size):
+            for c in range(plan.g):
+                out[(start + i) * plan.g + c] = values[
+                    i * plan.N : (i + 1) * plan.N, c * plan.N : (c + 1) * plan.N
+                ]
 
 
 def first_kernel(plan, field, z_fwd, y_fwd, out):
     x = pl.program_id(0)
-
-    @pl.when(x == 0)
-    def _():
-        out[:, :, plan.rows :, :] = jnp.zeros((M, plan.h, 8, 128), F32)
-
     lines_of(plan, lambda c: field[c, 0], x, z_fwd, y_fwd, out)
 
 
-def spread_weight(plan, weight, spread):
+def spread_weight(plan, weight, spread, transposed):
     rows = plan.C * T16
-    half = dot(spread[...], weight[...]).astype(BF)
-    full = dot_t(half, spread[...])
+    narrow = spread[...][:, : plan.C]
+    half = (dot_t if transposed else dot)(narrow, weight[...]).astype(BF)
+    full = dot_t(half, narrow)
     r = lax.broadcasted_iota(jnp.int32, (rows, rows), 0) % T16
     c = lax.broadcasted_iota(jnp.int32, (rows, rows), 1) % T16
     return jnp.where(r == c, full, 0.0)
@@ -157,7 +180,7 @@
     @pl.when(x == 0)
     def _():
         out[:, :, plan.rows :, :] = jnp.zeros((M, plan.h, 8, 128), F32)
-        mix[...] = spread_weight(plan, weight, spread).astype(BF)
+        mix[...] = spread_weight(plan, weight, spread, False).astype(BF)
         acc[...] = jnp.zeros_like(acc)
         bias_acc[...] = jnp.zeros_like(bias_acc)
 
@@ -205,7 +228,7 @@
 
     @pl.when(x == 0)
     def _():
-        mix[...] = spread_weight(plan, weight, spread).astype(BF)
+        mix[...] = spread_weight(plan, weight, spread, True).astype(BF)
 
     field_of(plan, lines, x, y_inv, z_inv, pre)
 
@@ -229,8 +252,8 @@
     return pl.BlockSpec((plan.C, 1, plan.N, plan.N), lambda x: (0, x, 0, 0))
 
 
-def lines_shape(plan):
-    return (M, plan.h, plan.rows_p, 128)
+def lines_shape(plan, spare=True):
+    return (M, plan.h, plan.rows_p if spare else plan.rows, 128)
 
 
 def run_first(plan, field):
@@ -239,15 +262,11 @@
         functools.partial(first_kernel, plan),
         grid=(plan.X,),
         in_specs=[plane_spec(plan)] + [whole(c.shape) for c in consts],
-        out_specs=whole(lines_shape(plan)),
-        out_shape=jax.ShapeDtypeStruct(lines_shape(plan), F32),
+        out_specs=whole(lines_shape(plan, False)),
+        out_shape=jax.ShapeDtypeStruct(lines_shape(plan, False), F32),
         compiler_params=params(),
         name="first",
     )(field, *[jnp.asarray(c) for c in consts])
-
-
-def pad_weight(weight):
-    return jnp.pad(weight, ((0, 128 - weight.shape[0]), (0, 128 - weight.shape[1])))
 
 
 def run_middle(plan, lines, field, cot, weight, bias):
@@ -258,8 +277,8 @@
         functools.partial(middle_kernel, plan),
         grid=(plan.X,),
         in_specs=[
-            whole(lines_shape(plan)), plane_spec(plan), plane_spec(plan),
-            whole((128, 128)), whole((plan.C, 1, 128)),
+            whole(lines_shape(plan, False)), plane_spec(plan), plane_spec(plan),
+            whole(weight.shape), whole((plan.C, 1, 128)),
         ] + [whole(c.shape) for c in consts],
         out_specs=(plane_spec(plan), whole(lines_shape(plan))),
         out_shape=(
@@ -274,7 +293,7 @@
         ],
         compiler_params=params(),
         name="middle",
-    )(lines, field, cot, pad_weight(weight), wide, *[jnp.asarray(c) for c in consts])
+    )(lines, field, cot, weight, wide, *[jnp.asarray(c) for c in consts])
 
 
 def run_last(plan, lines, slope, weight):
@@ -283,7 +302,7 @@
     return pl.pallas_call(
         functools.partial(last_kernel, plan),
         grid=(plan.X,),
-        in_specs=[whole(lines_shape(plan)), plane_spec(plan), whole((128, 128))]
+        in_specs=[whole(lines_shape(plan)), plane_spec(plan), whole(weight.shape)]
         + [whole(c.shape) for c in consts],
         out_specs=plane_spec(plan),
         out_shape=jax.ShapeDtypeStruct(slope.shape, BF),
@@ -293,7 +312,7 @@
         ],
         compiler_params=params(),
         name="last",
-    )(lines, slope, pad_weight(weight.T), *[jnp.asarray(c) for c in consts])
+    )(lines, slope, weight, *[jnp.asarray(c) for c in consts])
 
 
 def modes_of(plan, lines, x_fwd, fold):
@@ -349,7 +368,6 @@
 
     lax.fori_loop(0, modes.shape[0] // 64, chunk, 0)
     lines_back(plan, ab[0], ab[1], False, x_inv, unfold, out)
-    out[:, plan.rows :, :] = jnp.zeros((plan.S, 8, 128), F32)
 
 
 def mix_backward(plan, lines, weight, modes, x_fwd, x_inv, fold, unfold, e1, e2, e1t,
@@ -385,7 +403,7 @@
     return pl.pallas_call(
         functools.partial(mix_forward, plan),
         out_shape=(
-            jax.ShapeDtypeStruct((plan.S, plan.rows_p, 128), F32),
+            jax.ShapeDtypeStruct((plan.S, plan.rows, 128), F32),
             jax.ShapeDtypeStruct((rows, 256), BF),
         ),
         scratch_shapes=[pltpu.VMEM((2, rows, 128), BF)],
@@ -436,7 +454,7 @@
         copy.wait()
 
 
-def exchange(plan, blocks):
+def exchange(plan, blocks, call):
     n = plan.S
     return pl.pallas_call(
         functools.partial(exchange_kernel, n),
@@ -448,8 +466,8 @@
             pltpu.SemaphoreType.DMA((n,)),
             pltpu.SemaphoreType.DMA,
         ],
-        compiler_params=pltpu.CompilerParams(collective_id=0, has_side_effects=True),
-        name="exchange",
+        compiler_params=pltpu.CompilerParams(collective_id=call, has_side_effects=True),
+        name="exchange" + str(call),
     )(blocks)
 
 
@@ -458,13 +476,13 @@
     owners = (plan.S, plan.rows_p, 128)
     weight = spectral_weight.reshape(plan.kl * 2 * M, plan.pairs)
     lines = run_first(plan, inputs)
-    got = exchange(plan, lines.reshape(owners))
+    got = exchange(plan, lines.reshape(plan.S, plan.rows, 128), 0)
     back, modes = run_mix_forward(plan, got, weight)
-    got = exchange(plan, back).reshape(lines_shape(plan))
+    got = exchange(plan, back, 0).reshape(lines_shape(plan, False))
     slope, lines = run_middle(plan, got, inputs, cotangent, pointwise_weight, bias)
-    got = exchange(plan, lines.reshape(owners))
+    got = exchange(plan, lines.reshape(owners), 1)
     back, grad = run_mix_backward(plan, got, weight, modes)
-    got = exchange(plan, back)
+    got = exchange(plan, back, 1)
     grad_input = run_last(plan, got.reshape(lines_shape(plan)), slope, pointwise_weight)
     small = got[:, plan.rows : plan.rows + plan.rp, :].reshape(plan.S * plan.rp, 128)[:C]
     return (

time: 276 us -> 243 us (0.88)
  Pallas kernels: 257 us -> 227 us
  local copies, waits for them, and re-layouts: 14.6 us -> 11.8 us
    pallas_call x1, Pallas kernels: 80.7 us -> 67.2 us  [run_middle(): pl.pallas_call(functools.partial(middle_kernel, plan), grid=(plan.X,), in...]
    pallas_call x1, Pallas kernels: 37.7 us -> 28.4 us  [run_last(): pl.pallas_call(functools.partial(last_kernel, plan), grid=(plan.X,), in_s...]
    pallas_call x1, Pallas kernels: 17.8 us -> 13.5 us  [run_first(): pl.pallas_call(functools.partial(first_kernel, plan), grid=(plan.X,), in_...]
where the time goes in v2:
time: 243 us; the launch traced here: 239 us
  Pallas kernels  227 us (93%)
  local copies, waits for them, and re-layouts  11.8 us (5%)
    pallas_call x4, Pallas kernels, exchange(): pl.pallas_call(functools.partial(exchange_kernel, n), out_shape=jax.Shape...  87.7 us
    pallas_call x1, Pallas kernels, run_middle(): pl.pallas_call(functools.partial(middle_kernel, plan), grid=(plan.X,), in...  67.2 us
    pallas_call x1, Pallas kernels, run_last(): pl.pallas_call(functools.partial(last_kernel, plan), grid=(plan.X,), in_s...  28.4 us
    pallas_call x1, Pallas kernels, run_mix_backward(): pl.pallas_call(functools.partial(mix_backward, plan), out_shape=(jax.Shap...  16.4 us
    pallas_call x1, Pallas kernels, run_mix_forward(): pl.pallas_call(functools.partial(mix_forward, plan), out_shape=(jax.Shape...  13.6 us
    pallas_call x1, Pallas kernels, run_first(): pl.pallas_call(functools.partial(first_kernel, plan), grid=(plan.X,), in_...  13.5 us
    reshape x1, local copies, waits for them, and re-layouts, per_device(): grad.reshape(plan.kl, M, 2, plan.pairs)  6.42 us

profile of v2, /device:TPU:0, one launch (start us, length us, event | category | flops | bytes accessed | tf_op | source)
XLA Modules:
  0.0 239.3 jit_solution(5768943535504500208)
XLA Ops:
  0.6 0.0 copy-start
  0.6 1.5 broadcast_in_dim.2.bias
  2.2 13.5 %first.1 = f32[16,1,96,128]{3,2,1,0:T(8,128)} custom-call(bf16[48,8,128,128]{3,2,1,0:T(8,128)(2,1)} %field.3, bf16[512,256]{1,0:T(8,128)(2,1)} %constant.26.clone.z_fwd, bf16[16,256]{1,0:T(8,128)(2,1)} %constant.27.clone.y_fwd), custom_call_target="tpu_custom_call" | custom-call | tf_op jit(solution)/shard_map/first/pallas_call | solution.py:261
  15.7 19.8 %exchange0.2.lines = f32[16,96,128]{2,1,0:T(8,128)} custom-call(f32[16,96,128]{2,1,0:T(8,128)} %bitcast.6), custom_call_target="tpu_custom_call" | custom-call | tf_op jit(solution)/shard_map/exchange0/pallas_call | solution.py:459
  35.5 0.0 copy-done
  35.5 2.3 reshape.33.weight
  37.9 13.6 %mix_forward.1 = (f32[16,96,128]{2,1,0:T(8,128)}, bf16[512,256]{1,0:T(8,128)(2,1)}) custom-call(f32[16,96,128]{2,1,0:T(8,128)} %exchange0.2.lines, bf16[512,2304]{1,0:T(8,128)(2,1)} %reshape.33.weight, f32[64,128]{1,0:T(8,128)} %constant.28.clone.x_fwd, f32[128,64]{1,0:T(8,128)} %constant.29.clone.x_inv, bf16[1536,256]{1,0:T(8,128)(2,1)} %constant.30.clone.fold, ...), custom_call_target="tpu_custom_call" | custom-call | tf_op jit(solution)/shard_map/mix_forward/pallas_call | solution.py:403
  51.5 21.8 %exchange0.3 = f32[16,96,128]{2,1,0:T(8,128)} custom-call(f32[16,96,128]{2,1,0:T(8,128)} %get-tuple-element.10.src), custom_call_target="tpu_custom_call" | custom-call | tf_op jit(solution)/shard_map/exchange0/pallas_call | solution.py:459
  73.2 67.2 %middle.1 = (bf16[48,8,128,128]{3,2,1,0:T(8,128)(2,1)}, f32[16,1,104,128]{3,2,1,0:T(8,128)}) custom-call(f32[16,1,96,128]{3,2,1,0:T(8,128)} %bitcast.7, bf16[48,8,128,128]{3,2,1,0:T(8,128)(2,1)} %field.3, bf16[48,8,128,128]{3,2,1,0:T(8,128)(2,1)} %cot.1, bf16[48,48]{1,0:T(8,128)(2,1)} %weight.3, f32[48,1,128]{2,1,0:T(1,128)} %broadcast_in_dim.2.bias, ...), custom_call_target="tpu_custom_call" | custom-call | tf_op jit(solution)/shard_map/middle/pallas_call | solution.py:276
  140.5 22.9 %exchange1.2.lines = f32[16,104,128]{2,1,0:T(8,128)} custom-call(f32[16,104,128]{2,1,0:T(8,128)} %bitcast.8), custom_call_target="tpu_custom_call" | custom-call | tf_op jit(solution)/shard_map/exchange1/pallas_call | solution.py:459
  163.3 16.4 %mix_backward.1 = (f32[16,104,128]{2,1,0:T(8,128)}, f32[512,2304]{1,0:T(8,128)}) custom-call(f32[16,104,128]{2,1,0:T(8,128)} %exchange1.2.lines, bf16[512,2304]{1,0:T(8,128)(2,1)} %reshape.33.weight, bf16[512,256]{1,0:T(8,128)(2,1)} %get-tuple-element.12.modes, f32[64,128]{1,0:T(8,128)} %constant.28.clone.x_fwd, f32[128,64]{1,0:T(8,128)} %constant.29.clone.x_inv, ...), custom_call_target="tpu_custom_call" | custom-call | tf_op jit(solution)/shard_map/mix_backward/pallas_call | solution.py:418
  179.7 23.2 %exchange1.3 = f32[16,104,128]{2,1,0:T(8,128)} custom-call(f32[16,104,128]{2,1,0:T(8,128)} %get-tuple-element.13.src), custom_call_target="tpu_custom_call" | custom-call | tf_op jit(solution)/shard_map/exchange1/pallas_call | solution.py:459
  202.9 28.4 %last.1 = bf16[48,8,128,128]{3,2,1,0:T(8,128)(2,1)} custom-call(f32[16,1,104,128]{3,2,1,0:T(8,128)} %bitcast.5, bf16[48,8,128,128]{3,2,1,0:T(8,128)(2,1)} %get-tuple-element.14.slope, bf16[48,48]{1,0:T(8,128)(2,1)} %weight.3, bf16[768,128]{1,0:T(8,128)(2,1)} %constant.34.clone.spread, bf16[128,32]{1,0:T(8,128)(2,1)} %constant.35.clone.y_inv, ...), custom_call_target="tpu_custom_call" | custom-call | tf_op jit(solution)/shard_map/last/pallas_call | solution.py:302
  231.3 0.8 slice.9
  232.2 0.0 copy-start.1
  232.2 0.7 slice_reduce_fusion
  232.9 6.4 %reshape.37 = f32[16,16,2,2304]{3,2,1,0:T(2,128)} reshape(f32[512,2304]{1,0:T(8,128)} %get-tuple-element.15) | data formatting | bytes 9437184 | tf_op jit(solution)/shard_map/reshape | solution.py:490
  239.3 0.0 copy-done.1
  (1 shorter events, 0.0 us)
Async XLA Ops:
  0.6 34.9 %copy-start = (bf16[16,16,2,2304]{3,2,1,0:T(2,128)(2,1)S(1)}, bf16[16,16,2,2304]{3,2,1,0:T(2,128)(2,1)}, u32[]{:S(2)}) copy-start(bf16[16,16,2,2304]{3,2,1,0:T(2,128)(2,1)} %param.20) | copy-start | bytes 7077892
  232.2 7.1 %copy-start.1 = (f32[48,128]{1,0:T(8,128)}, f32[48,128]{1,0:T(8,128)S(1)}, u32[]{:S(2)}) copy-start(f32[48,128]{1,0:T(8,128)S(1)} %reshape.38) | copy-start | bytes 73732

commit v3 on v2

--- a/solution.py
+++ b/solution.py
@@ -199,7 +199,7 @@
             bias_acc[...] += wider[:, :8] + wider[:, 8:]
         return carry
 
-    lax.fori_loop(0, N // (2 * T16), block, 0)
+    lax.fori_loop(0, N // (2 * T16), block, 0, unroll=True)
     lines_of(plan, lambda c: slope[c, 0], x, z_fwd, y_fwd, out)
     tall = lambda ref: jnp.concatenate(
         [ref[:, 0, i * T16 : (i + 1) * T16, :].reshape(rows, N) for i in range(N // T16)], axis=1
@@ -241,7 +241,7 @@
             grad[:, 0, y, :] = (part + pre[:, y, :]).astype(BF)
         return carry
 
-    lax.fori_loop(0, N // (2 * T16), block, 0)
+    lax.fori_loop(0, N // (2 * T16), block, 0, unroll=True)
 
 
 def whole(shape):
@@ -366,7 +366,7 @@
             ab[part, rows, :] = dot((wide * w).astype(BF), e2t[...]).astype(BF)
         return carry
 
-    lax.fori_loop(0, modes.shape[0] // 64, chunk, 0)
+    lax.fori_loop(0, modes.shape[0] // 64, chunk, 0, unroll=2)
     lines_back(plan, ab[0], ab[1], False, x_inv, unfold, out)
 
 
@@ -391,7 +391,7 @@
         grad[rows, :] = first + ui * dot(turned[rows, 128:], e2[...])
         return carry
 
-    lax.fori_loop(0, s.shape[0] // 64, chunk, 0)
+    lax.fori_loop(0, s.shape[0] // 64, chunk, 0, unroll=2)
     lines_back(plan, ab[0], ab[1], True, x_inv, unfold, out)
     total = jnp.sum(lines[:, plan.rows :, :], axis=0) * float(plan.N) ** -1.5
     out[:, plan.rows :, :] = jnp.broadcast_to(total[None], (plan.S, 8, 128))

time: 243 us -> 232 us (0.955)
  Pallas kernels: 227 us -> 216 us
    pallas_call x1, Pallas kernels: 28.4 us -> 21.7 us  [run_last(): pl.pallas_call(functools.partial(last_kernel, plan), grid=(plan.X,), in_s...]
    pallas_call x1, Pallas kernels: 67.2 us -> 62.6 us  [run_middle(): pl.pallas_call(functools.partial(middle_kernel, plan), grid=(plan.X,), in...]
where the time goes in v3:
time: 232 us; the launch traced here: 228 us
  Pallas kernels  216 us (93%)
  local copies, waits for them, and re-layouts  11.8 us (5%)
    pallas_call x4, Pallas kernels, exchange(): pl.pallas_call(functools.partial(exchange_kernel, n), out_shape=jax.Shape...  87.6 us
    pallas_call x1, Pallas kernels, run_middle(): pl.pallas_call(functools.partial(middle_kernel, plan), grid=(plan.X,), in...  62.6 us
    pallas_call x1, Pallas kernels, run_last(): pl.pallas_call(functools.partial(last_kernel, plan), grid=(plan.X,), in_s...  21.7 us
    pallas_call x1, Pallas kernels, run_mix_backward(): pl.pallas_call(functools.partial(mix_backward, plan), out_shape=(jax.Shap...  17.3 us
    pallas_call x1, Pallas kernels, run_first(): pl.pallas_call(functools.partial(first_kernel, plan), grid=(plan.X,), in_...  13.5 us
    pallas_call x1, Pallas kernels, run_mix_forward(): pl.pallas_call(functools.partial(mix_forward, plan), out_shape=(jax.Shape...  13.1 us
    reshape x1, local copies, waits for them, and re-layouts, per_device(): grad.reshape(plan.kl, M, 2, plan.pairs)  6.42 us

profile of v3, /device:TPU:0, one launch (start us, length us, event | category | flops | bytes accessed | tf_op | source)
XLA Modules:
  0.0 228.3 jit_solution(9350857628794082433)
XLA Ops:
  0.6 0.0 copy-start
  0.6 1.5 broadcast_in_dim.2.bias
  2.2 13.5 %first.1 = f32[16,1,96,128]{3,2,1,0:T(8,128)} custom-call(bf16[48,8,128,128]{3,2,1,0:T(8,128)(2,1)} %field.3, bf16[512,256]{1,0:T(8,128)(2,1)} %constant.26.clone.z_fwd, bf16[16,256]{1,0:T(8,128)(2,1)} %constant.27.clone.y_fwd), custom_call_target="tpu_custom_call" | custom-call | tf_op jit(solution)/shard_map/first/pallas_call | solution.py:261
  15.7 19.8 %exchange0.2.lines = f32[16,96,128]{2,1,0:T(8,128)} custom-call(f32[16,96,128]{2,1,0:T(8,128)} %bitcast.6), custom_call_target="tpu_custom_call" | custom-call | tf_op jit(solution)/shard_map/exchange0/pallas_call | solution.py:459
  35.5 0.0 copy-done
  35.5 2.3 %reshape.33.weight = bf16[512,2304]{1,0:T(8,128)(2,1)} reshape(bf16[16,16,2,2304]{3,2,1,0:T(2,128)(2,1)S(1)} %copy-done) | data formatting | bytes 4718592 | tf_op jit(solution)/shard_map/reshape | solution.py:477
  37.9 13.1 %mix_forward.1 = (f32[16,96,128]{2,1,0:T(8,128)}, bf16[512,256]{1,0:T(8,128)(2,1)}) custom-call(f32[16,96,128]{2,1,0:T(8,128)} %exchange0.2.lines, bf16[512,2304]{1,0:T(8,128)(2,1)} %reshape.33.weight, f32[64,128]{1,0:T(8,128)} %constant.28.clone.x_fwd, f32[128,64]{1,0:T(8,128)} %constant.29.clone.x_inv, bf16[1536,256]{1,0:T(8,128)(2,1)} %constant.30.clone.fold, ...), custom_call_target="tpu_custom_call" | custom-call | tf_op jit(solution)/shard_map/mix_forward/pallas_call | solution.py:403
  51.0 21.8 %exchange0.3 = f32[16,96,128]{2,1,0:T(8,128)} custom-call(f32[16,96,128]{2,1,0:T(8,128)} %get-tuple-element.10.src), custom_call_target="tpu_custom_call" | custom-call | tf_op jit(solution)/shard_map/exchange0/pallas_call | solution.py:459
  72.7 62.6 %middle.1 = (bf16[48,8,128,128]{3,2,1,0:T(8,128)(2,1)}, f32[16,1,104,128]{3,2,1,0:T(8,128)}) custom-call(f32[16,1,96,128]{3,2,1,0:T(8,128)} %bitcast.7, bf16[48,8,128,128]{3,2,1,0:T(8,128)(2,1)} %field.3, bf16[48,8,128,128]{3,2,1,0:T(8,128)(2,1)} %cot.1, bf16[48,48]{1,0:T(8,128)(2,1)} %weight.3, f32[48,1,128]{2,1,0:T(1,128)} %broadcast_in_dim.2.bias, ...), custom_call_target="tpu_custom_call" | custom-call | tf_op jit(solution)/shard_map/middle/pallas_call | solution.py:276
  135.3 22.8 %exchange1.2.lines = f32[16,104,128]{2,1,0:T(8,128)} custom-call(f32[16,104,128]{2,1,0:T(8,128)} %bitcast.8), custom_call_target="tpu_custom_call" | custom-call | tf_op jit(solution)/shard_map/exchange1/pallas_call | solution.py:459
  158.1 17.3 %mix_backward.1 = (f32[16,104,128]{2,1,0:T(8,128)}, f32[512,2304]{1,0:T(8,128)}) custom-call(f32[16,104,128]{2,1,0:T(8,128)} %exchange1.2.lines, bf16[512,2304]{1,0:T(8,128)(2,1)} %reshape.33.weight, bf16[512,256]{1,0:T(8,128)(2,1)} %get-tuple-element.12.modes, f32[64,128]{1,0:T(8,128)} %constant.28.clone.x_fwd, f32[128,64]{1,0:T(8,128)} %constant.29.clone.x_inv, ...), custom_call_target="tpu_custom_call" | custom-call | tf_op jit(solution)/shard_map/mix_backward/pallas_call | solution.py:418
  175.5 23.2 %exchange1.3 = f32[16,104,128]{2,1,0:T(8,128)} custom-call(f32[16,104,128]{2,1,0:T(8,128)} %get-tuple-element.13.src), custom_call_target="tpu_custom_call" | custom-call | tf_op jit(solution)/shard_map/exchange1/pallas_call | solution.py:459
  198.6 21.7 %last.1 = bf16[48,8,128,128]{3,2,1,0:T(8,128)(2,1)} custom-call(f32[16,1,104,128]{3,2,1,0:T(8,128)} %bitcast.5, bf16[48,8,128,128]{3,2,1,0:T(8,128)(2,1)} %get-tuple-element.14.slope, bf16[48,48]{1,0:T(8,128)(2,1)} %weight.3, bf16[768,128]{1,0:T(8,128)(2,1)} %constant.34.clone.spread, bf16[128,32]{1,0:T(8,128)(2,1)} %constant.35.clone.y_inv, ...), custom_call_target="tpu_custom_call" | custom-call | tf_op jit(solution)/shard_map/last/pallas_call | solution.py:302
  220.3 0.8 slice.9
  221.2 0.0 copy-start.1
  221.2 0.7 slice_reduce_fusion
  221.9 6.4 %reshape.37 = f32[16,16,2,2304]{3,2,1,0:T(2,128)} reshape(f32[512,2304]{1,0:T(8,128)} %get-tuple-element.15) | data formatting | bytes 9437184 | tf_op jit(solution)/shard_map/reshape | solution.py:490
  228.3 0.0 copy-done.1
  (1 shorter events, 0.0 us)
Async XLA Ops:
  0.6 34.9 %copy-start = (bf16[16,16,2,2304]{3,2,1,0:T(2,128)(2,1)S(1)}, bf16[16,16,2,2304]{3,2,1,0:T(2,128)(2,1)}, u32[]{:S(2)}) copy-start(bf16[16,16,2,2304]{3,2,1,0:T(2,128)(2,1)} %param.20) | copy-start | bytes 7077892
  221.2 7.1 %copy-start.1 = (f32[48,128]{1,0:T(8,128)}, f32[48,128]{1,0:T(8,128)S(1)}, u32[]{:S(2)}) copy-start(f32[48,128]{1,0:T(8,128)S(1)} %reshape.38) | copy-start | bytes 73732
